TPU v7x, 256 devices: a whole 4x4x8 slice. The times are simulated.
256 devices in a mesh: dp: 32 (over z, x), seq: 8 (over y, core).
Axes of the slice: x: 4, y: 4, z: 8, core: 2. Of those that a mesh axis runs over, the one named last changes fastest.
Arguments:
- patches: bfloat16 [32, 98304], P(None, ('dp', 'seq')), may hold values from -12 to 12
- segment_ids: int32 [32, 3072], P('dp'), may hold values from 0 to 15, never falling along the last dimension, each value on 1 to 2304 neighbouring positions
- regroup_plan: int32 [32, 5, 64], P('dp'), may hold values from 0 to 383, as said below
- input_weight: bfloat16 [32, 1280], replicated, may hold values from -1 to 1
- input_bias: float32 [1280], replicated, may hold values from -3 to 3
- skip_weight: bfloat16 [32, 1280], replicated, may hold values from -1 to 1
- hidden_weight: bfloat16 [1280, 1280], replicated, may hold values from -0.15625 to 0.15625
- output_bias: float32 [1280], replicated, may hold values from -3 to 3
- norm_gain: float32 [1280], replicated, may hold values from 0.1 to 1.9
- head_scale: float32 [8], replicated, may hold values from 1 to 4
- qkv_weight: bfloat16 [1280, 3, 640], replicated, may hold values from -0.15625 to 0.15625
- out_weight: bfloat16 [640, 1280], P(None, ('dp', 'seq')), may hold values from -0.25 to 0.25
- cotangent: bfloat16 [98304, 1280], P(('dp', 'seq')), may hold values from -0.3125 to 0.3125
Outputs:
- layer_out: bfloat16 [98304, 1280], P(('dp', 'seq'))
- out_grad: float32 [640, 1280], P(None, ('dp', 'seq'))
Inputs may be any that keep to these rules, and one draw needn't show every extreme that they name: `regroup_plan`: piece s * 8 + d of a window moves rows of source shard s to destination shard d: one piece for each pair, each moving one row or more. The pieces of a window cover each of the 384 rows of every source shard once and each of the 384 rows of every destination shard once. A piece moves at most 96 rows, and in every window some piece moves exactly 96. `segment_ids`: series ids never fall along a window's positions; one series of each window has exactly 2304 positions.
All inputs are finite; a program needn't handle non-finite values.
Results may differ from a plain program's by a relative error of at most 0.015.
Values may be sent and summed in bfloat16 or wider, within the bound.
A program may use at most 64 MiB of HBM per device.

v0:
```python
import math
import jax
import jax.numpy as jnp
from jax import lax
from jax.sharding import PartitionSpec as P

HD = 80
EPSILON = 1e-06
CONTRACT_FIRST = (((0,), (0,)), ((), ()))


def row_norm(values):
    return values * lax.rsqrt(jnp.mean(values * values, axis=-1, keepdims=True) + EPSILON)


def place_table(plan_rows, shard_rows, shard_count):
    source = plan_rows[0]
    first_row = plan_rows[1]
    row_count = plan_rows[2]
    target = plan_rows[3]
    offset_row = plan_rows[4]
    window_len = shard_rows * shard_count
    loader_row = jnp.arange(window_len, dtype=jnp.int32)
    begin_row = source * shard_rows + first_row
    inside = (loader_row[None, :] >= begin_row[:, None]) & (
        loader_row[None, :] < (begin_row + row_count)[:, None]
    )
    earlier = (
        (source[:, None] == source[None, :])
        & (target[:, None] == target[None, :])
        & (first_row[None, :] < first_row[:, None])
    )
    base_rank = jnp.sum(jnp.where(earlier, row_count[None, :], 0), axis=1)
    position = jnp.sum(
        jnp.where(
            inside, (target * shard_rows + offset_row - begin_row)[:, None] + loader_row[None, :], 0
        ),
        axis=0,
    )
    slot_rank = jnp.sum(
        jnp.where(inside, (base_rank - begin_row)[:, None] + loader_row[None, :], 0), axis=0
    )
    return (position, slot_rank)


def patch_block(columns, input_weight, input_bias, skip_weight, hidden_weight, output_bias):
    pre_act = (
        lax.dot_general(columns, input_weight, CONTRACT_FIRST, preferred_element_type=jnp.float32)
        + input_bias
    )
    hidden = jax.nn.silu(pre_act).astype(jnp.bfloat16)
    skipped = lax.dot_general(
        columns, skip_weight, CONTRACT_FIRST, preferred_element_type=jnp.float32
    )
    embedded = (
        jnp.dot(hidden, hidden_weight, preferred_element_type=jnp.float32) + skipped + output_bias
    )
    return embedded.astype(jnp.bfloat16)


def per_device(
    patches,
    segment_ids,
    regroup_plan,
    input_weight,
    input_bias,
    skip_weight,
    hidden_weight,
    output_bias,
    norm_gain,
    head_scale,
    qkv_weight,
    out_weight,
    cotangent,
):
    shard_count = lax.axis_size("seq")
    shard_index = lax.axis_index("seq")
    shard_rows = cotangent.shape[0]
    model_width = cotangent.shape[1]
    window_len = shard_rows * shard_count
    capacity = 2 * shard_rows // shard_count
    position, slot_rank = place_table(regroup_plan[0], shard_rows, shard_count)
    loader_row = jnp.arange(window_len, dtype=jnp.int32)
    own_rows = lax.dynamic_slice_in_dim(position, shard_index * shard_rows, shard_rows, 0)
    own_ranks = lax.dynamic_slice_in_dim(slot_rank, shard_index * shard_rows, shard_rows, 0)
    send_slot = own_rows // shard_rows * capacity + own_ranks
    send_table = (
        jnp.full((shard_count * capacity,), shard_rows, jnp.int32)
        .at[send_slot]
        .set(jnp.arange(shard_rows, dtype=jnp.int32))
    )
    landing = jnp.where(position // shard_rows == shard_index, position % shard_rows, shard_rows)
    receive_table = (
        jnp.zeros((shard_rows,), jnp.int32)
        .at[landing]
        .set(loader_row // shard_rows * capacity + slot_rank, mode="drop")
    )
    local_embed = patch_block(
        patches, input_weight, input_bias, skip_weight, hidden_weight, output_bias
    )
    padded = jnp.concatenate([local_embed, jnp.zeros((1, model_width), jnp.bfloat16)], axis=0)
    arrived = lax.all_to_all(padded[send_table], "seq", split_axis=0, concat_axis=0, tiled=True)
    embedded = arrived[receive_table]
    normed = (row_norm(embedded.astype(jnp.float32)) * norm_gain).astype(jnp.bfloat16)
    projected = jnp.dot(
        normed, qkv_weight.reshape(model_width, -1), preferred_element_type=jnp.float32
    )
    projected = projected.astype(jnp.bfloat16).reshape(shard_rows, 3, -1)
    head_rows = lax.all_to_all(projected, "seq", split_axis=2, concat_axis=0, tiled=True)
    local_width = head_rows.shape[2]
    local_heads = local_width // HD
    queries = row_norm(
        head_rows[:, 0].reshape(window_len, local_heads, HD).astype(jnp.float32)
    ).astype(jnp.bfloat16)
    key_rows = row_norm(
        head_rows[:, 1].reshape(window_len, local_heads, HD).astype(jnp.float32)
    ).astype(jnp.bfloat16)
    value_rows = head_rows[:, 2].reshape(window_len, local_heads, HD)
    factor = lax.dynamic_slice_in_dim(head_scale, shard_index * local_heads, local_heads, 0) * (
        1.0 / math.sqrt(HD)
    )
    segment_row = segment_ids[0]
    block_len = min(512, window_len)
    block_count = window_len // block_len
    pieces = []
    for block_index in range(block_count):
        query_first = block_index * block_len
        query_part = queries[query_first : query_first + block_len]
        query_pos = query_first + jnp.arange(block_len, dtype=jnp.int32)
        query_seg = segment_row[query_first : query_first + block_len]
        key_len = query_first + block_len
        key_part = lax.slice_in_dim(key_rows, 0, key_len, axis=0)
        value_part = lax.slice_in_dim(value_rows, 0, key_len, axis=0)
        key_seg = lax.slice_in_dim(segment_row, 0, key_len, axis=0)
        key_pos = jnp.arange(key_len, dtype=jnp.int32)
        scores = (
            jnp.einsum("qhd,khd->hqk", query_part, key_part, preferred_element_type=jnp.float32)
            * factor[:, None, None]
        )
        allowed = (query_seg[:, None] == key_seg[None, :]) & (
            key_pos[None, :] <= query_pos[:, None]
        )
        weights = jnp.where(allowed[None], jnp.exp(scores), 0.0)
        summed = jnp.einsum(
            "hqk,khd->qhd",
            weights.astype(jnp.bfloat16),
            value_part,
            preferred_element_type=jnp.float32,
        )
        summed, denominator = (summed, jnp.sum(weights, axis=-1))
        pieces.append(
            (summed / jnp.transpose(denominator)[:, :, None]).reshape(block_len, local_width)
        )
    attended = jnp.concatenate(pieces, axis=0).astype(jnp.bfloat16)
    returned = lax.all_to_all(attended, "seq", split_axis=0, concat_axis=1, tiled=True)
    branch = jnp.dot(
        returned,
        lax.all_gather(out_weight, ("dp", "seq"), axis=1, tiled=True),
        preferred_element_type=jnp.float32,
    )
    layer_out = (embedded.astype(jnp.float32) + branch).astype(jnp.bfloat16)
    grad_term = lax.dot_general(
        returned, cotangent, CONTRACT_FIRST, preferred_element_type=jnp.float32
    )
    out_grad = lax.psum_scatter(grad_term, ("dp", "seq"), scatter_dimension=1, tiled=True)
    return (layer_out, out_grad)


def solution(mesh):
    placed = (
        P(None, ("dp", "seq")),
        P("dp", None),
        P("dp", None, None),
        P(),
        P(),
        P(),
        P(),
        P(),
        P(),
        P(),
        P(),
        P(None, ("dp", "seq")),
        P(("dp", "seq"), None),
    )
    return jax.shard_map(
        per_device,
        mesh=mesh,
        in_specs=placed,
        out_specs=(P(("dp", "seq"), None), P(None, ("dp", "seq"))),
        check_vma=False,
    )
```

profile of v0, /device:TPU:2, one launch (start us, length us, event | category | flops | bytes accessed | tf_op | source)
XLA Modules:
  0.0 472.5 jit_solution(12129723158445891963)
XLA Ops:
  7.2 0.0 copy-start
  7.2 0.9 slice_bitcast_fusion.37
  8.0 0.2 select_reduce_fusion.2
  8.2 0.7 fusion.119
  8.9 0.7 fusion.118
  9.6 0.4 select_reduce_fusion.1
  10.0 0.1 compare_select_fusion.4
  10.1 2.9 scatter_custom_fusion
  13.1 0.0 copy-done
  13.1 0.0 copy-start.4
  13.1 0.0 copy-start.5
  13.1 0.0 copy-start.6
  13.1 4.2 fusion.23
  17.3 0.0 copy-done.4
  17.3 0.0 copy-done.5
  17.3 0.0 copy-done.6
  17.3 2.0 fusion.9
  19.3 1.0 concatenate.7
  20.3 6.5 %gather_fusion = bf16[768,1280]{1,0:T(8,128)(2,1)} fusion(bf16[385,1280]{1,0:T(8,128)(2,1)} %concatenate.7, s32[1024]{0:T(1024)S(1)} %pad_clamp_fusion.1), kind=kCustom, calls=%fused_computation | custom fusion | bytes 3935232 | tf_op jit(solution)/shard_map/gather | solution.py:102
  26.8 4.5 all-to-all-start
  31.3 8.2 %copy.25 = bf16[1280,3,640]{0,2,1:T(8,128)(2,1)} copy(bf16[1280,3,640]{2,0,1:T(8,128)(2,1)} %param.23) | data formatting | bytes 9830400 | tf_op args[10]
  39.5 0.1 compare_select_fusion
  39.6 11.9 %scatter_custom_fusion.1 = s32[384]{0:T(512)S(1)} fusion(s32[3072]{0:T(1024)S(1)} %bitcast.265, s32[3072]{0:T(1024)S(1)} %get-tuple-element.36, s32[]{:T(128)} %constant.25.clone.1), kind=kCustom, calls=%fused_computation.154 | custom fusion | bytes 1540 | tf_op jit(solution)/shard_map/scatter | solution.py:96
  51.6 5.6 %all-to-all-done = bf16[8,96,1280]{2,1,0:T(8,128)(2,1)} async-done(((bf16[8,96,1280]{2,1,0:T(8,128)(2,1)}), bf16[8,96,1280]{2,1,0:T(8,128)(2,1)}, u32[]{:S(2)}, u32[]{:S(2)}) %all-to-all-start) | async-done | bytes 1966112 | tf_op jit(solution)/shard_map/all_to_all | solution.py:102
  57.2 5.6 %gather_fusion.1 = bf16[384,1280]{1,0:T(8,128)(2,1)} fusion(bf16[768,1280]{1,0:T(8,128)(2,1)} %bitcast.6, s32[1024]{0:T(1024)S(1)} %pad_clamp_fusion), kind=kCustom, calls=%fused_computation.1 | custom fusion | bytes 1967616 | tf_op jit(solution)/shard_map/gather | solution.py:103
  62.8 1.5 fusion.16
  64.3 6.2 %convolution_convert_fusion = bf16[384,1920]{1,0:T(8,128)(2,1)} fusion(bf16[1280,1920]{0,1:T(8,128)(2,1)} %bitcast.255, bf16[384,1280]{1,0:T(8,128)(2,1)} %gather_fusion.1, f32[1280]{0:T(1024)S(1)} %copy-done.7, f32[384]{0:T(512)S(1)} %add_rsqrt_fusion.2), kind=kOutput, calls=%fused_computation.27 | convolution fusion | flops 1890140160 | bytes 7379456 | tf_op jit(solution)/shard_map/dot_general | solution.py:105
  70.5 2.6 copy.26
  73.0 3.9 copy.27
  77.0 4.5 all-to-all-start.1
  81.4 0.0 all-gather.3.cloned.1.call-start
  81.5 0.7 all-gather.3.cloned.1.call-update
  82.2 0.3 all-reduce.4.cloned.1.call-start
  82.4 0.6 dynamic_slice.11
  83.8 23.4 %all-to-all-done.1 = bf16[384,3,640]{0,1,2:T(4,128)(2,1)} async-done(((bf16[384,3,640]{0,1,2:T(4,128)(2,1)}), bf16[384,3,640]{0,1,2:T(4,128)(2,1)}, u32[]{:S(2)}, u32[]{:S(2)}) %all-to-all-start.1) | async-done | bytes 1474592 | tf_op jit(solution)/shard_map/all_to_all | solution.py:109
  107.3 1.7 copy.28
  109.0 0.3 copy.32
  109.3 0.2 fusion.94
  109.5 0.2 fusion.95
  109.7 0.0 slice-start
  109.7 0.4 fusion.121
  110.2 0.2 fusion.91
  110.4 0.0 slice-done
  110.4 0.9 fusion.122
  111.4 1.4 fusion.123
  112.7 0.5 fusion.87
  113.2 0.6 fusion.63
  113.8 1.9 fusion.124
  115.7 0.8 fusion.81
  116.5 2.3 fusion.125
  118.8 0.9 fusion.75
  119.8 2.7 fusion.126
  122.5 0.0 copy-start.2
  122.5 1.1 fusion.69
  123.6 0.1 copy.34
  123.6 12.4 %all_to_all.46 = bf16[8,384,80]{1,2,0:T(8,128)(2,1)S(1)} all-to-all(bf16[8,384,80]{1,2,0:T(8,128)(2,1)S(1)} %bitcast.258), channel_id=1, replica_groups=mesh['dp'=32,'seq'=8] {'seq'}, dimensions={0} | all-to-all | bytes 983040 | tf_op jit(solution)/shard_map/all_to_all | solution.py:155
  136.1 0.8 copy-done.1
  136.9 2.9 fusion.127
  139.7 0.0 all-reduce.4.cloned.1.call-update
  139.7 54.4 %all-gather.3.cloned.1.call-done = bf16[256,5,640]{2,1,0:T(8,128)(2,1)} async-done(((bf16[1,5,640]{2,1,0:T(8,128)(2,1)}), bf16[256,5,640]{2,1,0:T(8,128)(2,1)}) %all-gather.3.cloned.1.call-update) | async-done | bytes 1638416 | tf_op jit(solution)/shard_map/all_gather | solution.py:158
  194.1 4.1 reshape.456
  198.2 3.8 fusion.10
  202.0 262.3 %all-reduce.4.cloned.1.call-done = f32[640,1280]{0,1:T(8,128)} async-done(((f32[640,1280]{0,1:T(8,128)}), f32[640,1280]{0,1:T(8,128)}) %all-reduce.4.cloned.1.call-update) | async-done | bytes 3276816
  464.3 1.4 constant_dynamic-slice_fusion
  (28 shorter events, 0.2 us)
Async XLA Ops:
  7.2 5.9 %copy-start = (bf16[1280,1280]{1,0:T(8,128)(2,1)S(1)}, bf16[1280,1280]{1,0:T(8,128)(2,1)}, u32[]{:S(2)}) copy-start(bf16[1280,1280]{1,0:T(8,128)(2,1)} %param.19) | copy-start | bytes 9830404
  13.1 4.2 copy-start.4
  13.1 4.2 copy-start.5
  13.1 4.2 copy-start.6
  26.8 30.4 %all-to-all-start = ((bf16[8,96,1280]{2,1,0:T(8,128)(2,1)}), bf16[8,96,1280]{2,1,0:T(8,128)(2,1)}, u32[]{:S(2)}, u32[]{:S(2)}) async-start(bf16[8,96,1280]{2,1,0:T(8,128)(2,1)} %bitcast.252), calls=%async_computation | async-start | bytes 3932160 | tf_op jit(solution)/shard_map/all_to_all | solution.py:102
  57.2 7.1 %copy-start.7 = (f32[1280]{0:T(1024)S(1)}, f32[1280]{0:T(1024)}, u32[]{:S(2)}) copy-start(f32[1280]{0:T(1024)} %param.21) | copy-start | bytes 15364
  76.9 5.5 %copy-start.8 = (f32[8]{0:T(128)S(1)}, f32[8]{0:T(128)}, u32[]{:S(2)}) copy-start(f32[8]{0:T(128)} %param.22) | copy-start | bytes 100
  76.9 6.8 %copy-start.3 = (s32[1,3072]{1,0:T(1,128)S(1)}, s32[1,3072]{1,0:T(1,128)}, u32[]{:S(2)}) copy-start(s32[1,3072]{1,0:T(1,128)} %param.14) | copy-start | bytes 36868
  77.0 30.3 %all-to-all-start.1 = ((bf16[384,3,640]{0,1,2:T(4,128)(2,1)}), bf16[384,3,640]{0,1,2:T(4,128)(2,1)}, u32[]{:S(2)}, u32[]{:S(2)}) async-start(bf16[384,3,640]{0,1,2:T(4,128)(2,1)} %copy.27), calls=%async_computation.1 | async-start | bytes 3932160 | tf_op jit(solution)/shard_map/all_to_all | solution.py:109
  81.4 112.7 %all-gather.3.cloned.1.call-start = ((), (), s32[]{:S(2)}) async-start(), calls=%async_computation.3 | async-start | bytes 2631680 | tf_op jit(solution)/shard_map/all_gather | solution.py:158
  82.2 382.1 %all-reduce.4.cloned.1.call-start = ((), (), s32[]{:S(2)}) async-start(), calls=%async_computation.4 | async-start | bytes 6553600
  109.7 0.7 slice-start
  112.7 1.1 slice-start.1
  122.5 14.4 %copy-start.2 = (bf16[384,1280]{1,0:T(8,128)(2,1)S(1)}, bf16[384,1280]{1,0:T(8,128)(2,1)}, u32[]{:S(2)}) copy-start(bf16[384,1280]{1,0:T(8,128)(2,1)} %param.25) | copy-start | bytes 2949124
  136.1 0.8 copy-start.1
Sparse Core Ops, SparseCore 0:
  86.0 108.0 all-gather.2
  199.6 264.6 all-reduce.3
where the time goes:
time: 474 us; the launch traced here: 473 us
  waiting for transfers between devices  346 us (73%)
  local copies, waits for them, and re-layouts  52.6 us (11%)
  matrix products  32.7 us (7%)
  between operations  15 us (3%)
  blocking collectives  12.4 us (3%)
  starting transfers between devices  9.23 us (2%)
    unnamed x3, waiting for transfers between devices  263 us
    all_gather x1, waiting for transfers between devices, per_device(): lax.all_gather(out_weight, ('dp', 'seq'), axis=1, tiled=True)  54.4 us
    all_to_all x1, waiting for transfers between devices, per_device(): lax.all_to_all(projected, 'seq', split_axis=2, concat_axis=0, tiled=True)  23.4 us
    unnamed x21, local copies, waits for them, and re-layouts  14.5 us
    all_to_all x1, blocking collectives, per_device(): lax.all_to_all(attended, 'seq', split_axis=0, concat_axis=1, tiled=True)  12.4 us
    scatter x1, local copies, waits for them, and re-layouts, per_device(): receive_table = jnp.zeros((shard_rows,), jnp.int32).at[landing].set(loade...  11.9 us
    dot_general x6, matrix products, per_device(): jnp.einsum('qhd,khd->hqk', query_part, key_part, preferred_element_type=j...  9.69 us
  transfers between devices with their start and end apart: 4, of which 4 were waited for; matrix products, arithmetic and copies ran while one was open for 10% of the time, Pallas kernels for 0%

commit v1 on v0

--- a/solution.py
+++ b/solution.py
@@ -7,6 +7,30 @@
 HD = 80
 EPSILON = 1e-06
 CONTRACT_FIRST = (((0,), (0,)), ((), ()))
+
+
+def cut_along(value, dim, devices):
+    lengths = value.shape
+    parts = value.reshape(*lengths[:dim], devices, lengths[dim] // devices, *lengths[dim + 1 :])
+    return jnp.moveaxis(parts, dim, 0)
+
+
+def in_order(blocks, dim):
+    lengths = list(blocks.shape[1:])
+    lengths[dim] *= blocks.shape[0]
+    return jnp.moveaxis(blocks, 0, dim).reshape(lengths)
+
+
+def rotated_exchange(array, axis, split_dim, concat_dim):
+    size, place = (lax.axis_size(axis), lax.axis_index(axis))
+    blocks = cut_along(array, split_dim, size)
+    result = blocks
+    for step in range(1, size):
+        target, source = ((place + step) % size, (place - step) % size)
+        sent = lax.dynamic_index_in_dim(blocks, target, 0)
+        received = lax.ppermute(sent, axis, [(i, (i + step) % size) for i in range(size)])
+        result = lax.dynamic_update_slice_in_dim(result, received, source, axis=0)
+    return in_order(result, concat_dim)
 
 
 def row_norm(values):
@@ -106,7 +130,7 @@
         normed, qkv_weight.reshape(model_width, -1), preferred_element_type=jnp.float32
     )
     projected = projected.astype(jnp.bfloat16).reshape(shard_rows, 3, -1)
-    head_rows = lax.all_to_all(projected, "seq", split_axis=2, concat_axis=0, tiled=True)
+    head_rows = rotated_exchange(projected, "seq", 2, 0)
     local_width = head_rows.shape[2]
     local_heads = local_width // HD
     queries = row_norm(

time: 474 us -> 427 us (0.901)
  waiting for transfers between devices: 346 us -> 299 us
    all_gather x1, waiting for transfers between devices: 54.4 us -> 20.3 us  [per_device(): lax.all_gather(out_weight, ('dp', 'seq'), axis=1, tiled=True)]
    all_to_all x1 -> x0, waiting for transfers between devices: 23.4 us -> none  [per_device(): lax.all_to_all(projected, 'seq', split_axis=2, concat_axis=0, tiled=True)]
    ppermute x0 -> x7, waiting for transfers between devices: none -> 12.4 us  [rotated_exchange(): lax.ppermute(sent, axis, [(i, (i + step) % size) for i in range(size)])]
    ppermute x0 -> x7, starting transfers between devices: none -> 7.83 us  [rotated_exchange(): lax.ppermute(sent, axis, [(i, (i + step) % size) for i in range(size)])]
    unnamed x21 -> x23, local copies, waits for them, and re-layouts: 14.5 us -> 14.6 us
  transfers between devices with their start and end apart: 4 -> 10, of which waited for: 4 -> 10; matrix products, arithmetic and copies ran while one was open for 10% -> 15% of each run, Pallas kernels for 0% -> 0%
where the time goes in v1:
time: 427 us
  waiting for transfers between devices  299 us (70%)
  local copies, waits for them, and re-layouts  48.6 us (11%)
  matrix products  32.7 us (8%)
  between operations  15.4 us (4%)
  blocking collectives  14.3 us (3%)
  starting transfers between devices  12.4 us (3%)
    unnamed x3, waiting for transfers between devices  263 us
    all_gather x1, waiting for transfers between devices, per_device(): lax.all_gather(out_weight, ('dp', 'seq'), axis=1, tiled=True)  20.3 us
    unnamed x23, local copies, waits for them, and re-layouts  14.6 us
    all_to_all x1, blocking collectives, per_device(): lax.all_to_all(attended, 'seq', split_axis=0, concat_axis=1, tiled=True)  14.3 us
    ppermute x7, waiting for transfers between devices, rotated_exchange(): lax.ppermute(sent, axis, [(i, (i + step) % size) for i in range(size)])  12.4 us
    scatter x1, local copies, waits for them, and re-layouts, per_device(): receive_table = jnp.zeros((shard_rows,), jnp.int32).at[landing].set(loade...  11.8 us
    dot_general x6, matrix products, per_device(): jnp.einsum('qhd,khd->hqk', query_part, key_part, preferred_element_type=j...  9.7 us
  transfers between devices with their start and end apart: 10, of which 10 were waited for; matrix products, arithmetic and copies ran while one was open for 15% of the time, Pallas kernels for 0%

profile of v1, /device:TPU:2, one launch (start us, length us, event | category | flops | bytes accessed | tf_op | source)
XLA Modules:
  0.0 426.6 jit_solution(8471343492828350736)
XLA Ops:
  7.2 0.9 slice_bitcast_fusion.37
  8.0 0.2 select_reduce_fusion.2
  8.2 0.7 fusion.119
  8.9 0.7 fusion.118
  9.6 0.4 select_reduce_fusion.1
  10.0 0.1 compare_select_fusion.4
  10.1 2.9 scatter_custom_fusion
  13.1 4.2 fusion.23
  17.3 2.0 fusion.9
  19.3 1.0 concatenate.7
  20.3 6.5 %gather_fusion = bf16[768,1280]{1,0:T(8,128)(2,1)} fusion(bf16[385,1280]{1,0:T(8,128)(2,1)} %concatenate.7, s32[1024]{0:T(1024)S(1)} %pad_clamp_fusion.1), kind=kCustom, calls=%fused_computation | custom fusion | bytes 3935232 | tf_op jit(solution)/shard_map/gather | solution.py:126
  26.8 4.5 %all-to-all-start = ((bf16[8,96,1280]{2,1,0:T(8,128)(2,1)}), bf16[8,96,1280]{2,1,0:T(8,128)(2,1)}, u32[]{:S(2)}, u32[]{:S(2)}) async-start(bf16[8,96,1280]{2,1,0:T(8,128)(2,1)} %bitcast.268), calls=%async_computation | async-start | bytes 3932160 | tf_op jit(solution)/shard_map/all_to_all | solution.py:126
  31.3 0.0 all-gather.3.cloned.1.call-start
  31.4 0.7 all-gather.3.cloned.1.call-update
  32.0 0.0 all-reduce.4.cloned.1.call-start
  32.4 8.2 %copy.23 = bf16[1280,3,640]{0,2,1:T(8,128)(2,1)} copy(bf16[1280,3,640]{2,0,1:T(8,128)(2,1)} %param.23) | data formatting | bytes 9830400 | tf_op args[10]
  40.6 0.6 dynamic_slice.40
  41.8 0.1 compare_select_fusion
  41.9 11.8 %scatter_custom_fusion.1 = s32[384]{0:T(512)S(1)} fusion(s32[3072]{0:T(1024)S(1)} %bitcast.279, s32[3072]{0:T(1024)S(1)} %get-tuple-element.43, s32[]{:T(128)} %constant.151.clone.1), kind=kCustom, calls=%fused_computation.168 | custom fusion | bytes 1540 | tf_op jit(solution)/shard_map/scatter | solution.py:120
  53.9 3.4 all-to-all-done
  57.3 5.6 %gather_fusion.1 = bf16[384,1280]{1,0:T(8,128)(2,1)} fusion(bf16[768,1280]{1,0:T(8,128)(2,1)} %bitcast.6, s32[1024]{0:T(1024)S(1)} %pad_clamp_fusion), kind=kCustom, calls=%fused_computation.1 | custom fusion | bytes 1967616 | tf_op jit(solution)/shard_map/gather | solution.py:127
  62.9 1.5 fusion.16
  64.3 6.1 %convolution_convert_fusion = bf16[384,1920]{1,0:T(8,128)(2,1)} fusion(bf16[1280,1920]{0,1:T(8,128)(2,1)} %bitcast.269, bf16[384,1280]{1,0:T(8,128)(2,1)} %gather_fusion.1, f32[1280]{0:T(1024)S(1)} %copy-done.8, f32[384]{0:T(512)S(1)} %add_rsqrt_fusion.2), kind=kOutput, calls=%fused_computation.27 | convolution fusion | flops 1890140160 | bytes 7379456 | tf_op jit(solution)/shard_map/dot_general | solution.py:129
  70.5 2.6 copy.24
  73.0 1.6 dynamic-slice_bitcast_fusion
  74.6 0.0 collective-permute-start
  74.7 0.8 collective-permute-start.1
  75.5 1.2 collective-permute-start.2
  76.7 2.7 collective-permute-start.3
  79.4 1.1 collective-permute-start.4
  80.5 1.4 collective-permute-done
  82.0 1.6 collective-permute-done.1
  83.6 2.0 collective-permute-start.6
  85.6 3.9 collective-permute-done.2
  89.6 1.7 collective-permute-done.3
  91.3 0.4 collective-permute-done.4
  91.7 1.1 collective-permute-done.5
  92.9 2.2 collective-permute-done.6
  95.2 0.2 copy.28
  95.4 0.2 fusion.94
  95.7 0.2 fusion.95
  95.9 0.4 fusion.121
  96.3 0.2 fusion.91
  96.5 0.0 slice-done
  96.6 0.9 fusion.122
  97.5 1.4 fusion.123
  98.9 0.5 fusion.87
  99.3 0.6 fusion.63
  99.9 1.9 fusion.124
  101.9 0.8 fusion.81
  102.7 2.3 fusion.125
  105.0 0.9 fusion.75
  105.9 2.7 fusion.126
  108.6 1.1 fusion.69
  109.7 0.1 copy.30
  109.8 14.3 %all_to_all.28 = bf16[8,384,80]{1,2,0:T(8,128)(2,1)S(1)} all-to-all(bf16[8,384,80]{1,2,0:T(8,128)(2,1)S(1)} %bitcast.272), channel_id=1, replica_groups=mesh['dp'=32,'seq'=8] {'seq'}, dimensions={0} | all-to-all | bytes 983040 | tf_op jit(solution)/shard_map/all_to_all | solution.py:179
  124.0 0.8 copy-done.2
  124.8 2.9 fusion.127
  127.8 0.0 all-reduce.4.cloned.1.call-update
  127.8 20.3 %all-gather.3.cloned.1.call-done = bf16[256,5,640]{2,1,0:T(8,128)(2,1)} async-done(((bf16[1,5,640]{2,1,0:T(8,128)(2,1)}), bf16[256,5,640]{2,1,0:T(8,128)(2,1)}) %all-gather.3.cloned.1.call-update) | async-done | bytes 1638416 | tf_op jit(solution)/shard_map/all_gather | solution.py:182
  148.0 4.1 reshape.463
  152.1 3.8 fusion.10
  155.9 262.5 %all-reduce.4.cloned.1.call-done = f32[640,1280]{0,1:T(8,128)} async-done(((f32[640,1280]{0,1:T(8,128)}), f32[640,1280]{0,1:T(8,128)}) %all-reduce.4.cloned.1.call-update) | async-done | bytes 3276816
  418.4 1.4 constant_dynamic-slice_fusion
  (48 shorter events, 0.4 us)
Async XLA Ops:
  7.2 5.9 %copy-start = (bf16[1280,1280]{1,0:T(8,128)(2,1)S(1)}, bf16[1280,1280]{1,0:T(8,128)(2,1)}, u32[]{:S(2)}) copy-start(bf16[1280,1280]{1,0:T(8,128)(2,1)} %param.19) | copy-start | bytes 9830404
  13.1 4.2 copy-start.5
  13.1 4.2 copy-start.6
  13.1 4.2 copy-start.7
  26.8 30.4 %all-to-all-start = ((bf16[8,96,1280]{2,1,0:T(8,128)(2,1)}), bf16[8,96,1280]{2,1,0:T(8,128)(2,1)}, u32[]{:S(2)}, u32[]{:S(2)}) async-start(bf16[8,96,1280]{2,1,0:T(8,128)(2,1)} %bitcast.268), calls=%async_computation | async-start | bytes 3932160 | tf_op jit(solution)/shard_map/all_to_all | solution.py:126
  31.3 116.7 %all-gather.3.cloned.1.call-start = ((), (), s32[]{:S(2)}) async-start(), calls=%async_computation.2 | async-start | bytes 2631680 | tf_op jit(solution)/shard_map/all_gather | solution.py:182
  32.0 386.3 %all-reduce.4.cloned.1.call-start = ((), (), s32[]{:S(2)}) async-start(), calls=%async_computation.3 | async-start | bytes 6553600
  32.4 8.2 %copy-start.9 = (f32[8]{0:T(128)S(1)}, f32[8]{0:T(128)}, u32[]{:S(2)}) copy-start(f32[8]{0:T(128)} %param.22) | copy-start | bytes 100
  32.4 21.4 %copy-start.4 = (s32[1,3072]{1,0:T(1,128)S(1)}, s32[1,3072]{1,0:T(1,128)}, u32[]{:S(2)}) copy-start(s32[1,3072]{1,0:T(1,128)} %param.14) | copy-start | bytes 36868
  57.2 7.1 %copy-start.8 = (f32[1280]{0:T(1024)S(1)}, f32[1280]{0:T(1024)}, u32[]{:S(2)}) copy-start(f32[1280]{0:T(1024)} %param.21) | copy-start | bytes 15364
  73.0 8.9 %copy-start.1 = (bf16[384,1920]{0,1:T(8,128)(2,1)S(1)}, bf16[384,1920]{0,1:T(8,128)(2,1)}, u32[]{:S(2)}) copy-start(bf16[384,1920]{0,1:T(8,128)(2,1)} %copy.24) | copy-start | bytes 4423684
  74.6 7.3 %collective-permute-start = (bf16[1,384,3,80]{1,3,0,2:T(8,128)(2,1)S(1)}, bf16[1,384,3,80]{1,3,0,2:T(8,128)(2,1)S(1)}, u32[]{:S(2)}, u32[]{:S(2)}) collective-permute-start(bf16[1,384,3,80]{1,3,0,2:T(8,128)(2,1)S(1)} %get-tuple-element.16), channel_id=1, source_target_pairs={{0,1},{1,2},{2,3},{3,4},{4,5},{5,6},{6,7},{7,0},{8,9},{9,10},{10,1... | collective-permute-start | bytes 552968 | tf_op jit(solution)/shard_map/ppermute | solution.py:31
  74.7 9.0 %collective-permute-start.1 = (bf16[1,384,3,80]{1,3,0,2:T(8,128)(2,1)S(1)}, bf16[1,384,3,80]{1,3,0,2:T(8,128)(2,1)S(1)}, u32[]{:S(2)}, u32[]{:S(2)}) collective-permute-start(bf16[1,384,3,80]{1,3,0,2:T(8,128)(2,1)S(1)} %get-tuple-element.15), channel_id=1, source_target_pairs={{0,2},{1,3},{2,4},{3,5},{4,6},{5,7},{6,0},{7,1},{8,10},{9,11},{10,... | collective-permute-start | bytes 552968 | tf_op jit(solution)/shard_map/ppermute | solution.py:31
  75.5 14.0 %collective-permute-start.2 = (bf16[1,384,3,80]{1,3,0,2:T(8,128)(2,1)S(1)}, bf16[1,384,3,80]{1,3,0,2:T(8,128)(2,1)S(1)}, u32[]{:S(2)}, u32[]{:S(2)}) collective-permute-start(bf16[1,384,3,80]{1,3,0,2:T(8,128)(2,1)S(1)} %get-tuple-element.14), channel_id=1, source_target_pairs={{0,3},{1,4},{2,5},{3,6},{4,7},{5,0},{6,1},{7,2},{8,11},{9,12},{10,... | collective-permute-start | bytes 552968 | tf_op jit(solution)/shard_map/ppermute | solution.py:31
  76.7 14.6 %collective-permute-start.3 = (bf16[1,384,3,80]{1,3,0,2:T(8,128)(2,1)S(1)}, bf16[1,384,3,80]{1,3,0,2:T(8,128)(2,1)S(1)}, u32[]{:S(2)}, u32[]{:S(2)}) collective-permute-start(bf16[1,384,3,80]{1,3,0,2:T(8,128)(2,1)S(1)} %get-tuple-element.13), channel_id=1, source_target_pairs={{0,4},{1,5},{2,6},{3,7},{4,0},{5,1},{6,2},{7,3},{8,12},{9,13},{10,... | collective-permute-start | bytes 552968 | tf_op jit(solution)/shard_map/ppermute | solution.py:31
  79.4 12.3 %collective-permute-start.4 = (bf16[1,384,3,80]{1,3,0,2:T(8,128)(2,1)S(1)}, bf16[1,384,3,80]{1,3,0,2:T(8,128)(2,1)S(1)}, u32[]{:S(2)}, u32[]{:S(2)}) collective-permute-start(bf16[1,384,3,80]{1,3,0,2:T(8,128)(2,1)S(1)} %get-tuple-element.12), channel_id=1, source_target_pairs={{0,5},{1,6},{2,7},{3,0},{4,1},{5,2},{6,3},{7,4},{8,13},{9,14},{10,... | collective-permute-start | bytes 552968 | tf_op jit(solution)/shard_map/ppermute | solution.py:31
  82.0 10.9 %collective-permute-start.5 = (bf16[1,384,3,80]{1,3,0,2:T(8,128)(2,1)S(1)}, bf16[1,384,3,80]{1,3,0,2:T(8,128)(2,1)S(1)}, u32[]{:S(2)}, u32[]{:S(2)}) collective-permute-start(bf16[1,384,3,80]{1,3,0,2:T(8,128)(2,1)S(1)} %get-tuple-element.11), channel_id=1, source_target_pairs={{0,6},{1,7},{2,0},{3,1},{4,2},{5,3},{6,4},{7,5},{8,14},{9,15},{10,... | collective-permute-start | bytes 552968 | tf_op jit(solution)/shard_map/ppermute | solution.py:31
  83.6 11.5 %collective-permute-start.6 = (bf16[1,384,3,80]{1,3,0,2:T(8,128)(2,1)S(1)}, bf16[1,384,3,80]{1,3,0,2:T(8,128)(2,1)S(1)}, u32[]{:S(2)}, u32[]{:S(2)}) collective-permute-start(bf16[1,384,3,80]{1,3,0,2:T(8,128)(2,1)S(1)} %get-tuple-element.10), channel_id=1, source_target_pairs={{0,7},{1,0},{2,1},{3,2},{4,3},{5,4},{6,5},{7,6},{8,15},{9,8},{10,9... | collective-permute-start | bytes 552968 | tf_op jit(solution)/shard_map/ppermute | solution.py:31
  95.9 0.7 slice-start
  98.9 1.1 slice-start.1
  108.6 16.2 %copy-start.3 = (bf16[384,1280]{1,0:T(8,128)(2,1)S(1)}, bf16[384,1280]{1,0:T(8,128)(2,1)}, u32[]{:S(2)}) copy-start(bf16[384,1280]{1,0:T(8,128)(2,1)} %param.25) | copy-start | bytes 2949124
  124.0 0.8 copy-start.2
Sparse Core Ops, SparseCore 0:
  35.9 112.1 all-gather.2
  153.5 264.8 all-reduce.3
